TPU v7x, 32 devices: a whole 2x2x4 slice. The times are simulated.
32 devices in a mesh: row: 8 (over y, x, core), col: 4 (over z).
Axes of the slice: x: 2, y: 2, z: 4, core: 2. Of those that a mesh axis runs over, the one named last changes fastest.
Arguments:
- harmonic: int32 [4, 1024], P('col', 'row'), may hold values from 0 to 312, as said below
- legendre: float32 [2, 4, 1024, 512], P(None, 'col', 'row'), may hold values from -6 to 6
- whitening: float32 [2, 512, 512], replicated
- longitude: float32 [2, 512], replicated, may hold values from -3.140625 to 3.140625
- observed: float32 [2, 512], replicated, may hold values from -6 to 6
Outputs:
- normal: float32 [4096, 4096], P('row', 'col')
- rhs: float32 [4, 1024], P('col', 'row')
Inputs may be any that keep to these rules, and one draw needn't show every extreme that they name: `harmonic`: A value is m for a cosine column and 156 + m for a sine column (m >= 1); the columns are the first 4095 coefficients of the list ordered by degree up to 156, together with the sine coefficient of degree and order 156, each once, in a random order.
All inputs are finite; a program needn't handle non-finite values.
Results may differ from a plain program's by a relative error of at most 0.00009.
Values sent between devices are 32-bit elements; how exact they have to be, the bound alone decides.
A program may use at most 64 MiB of HBM per device.

v0:
```python
import jax
import jax.numpy as jnp
from jax import lax
from jax.sharding import PartitionSpec as P

LMAX = 156


def from_root(value, axis, source):
    kept = jnp.where(lax.axis_index(axis) == source, value, 0).astype(value.dtype)
    return lax.psum(kept, axis)


def form_columns(azimuth, leg_values, whitening, longitude):
    is_cosine = azimuth <= LMAX
    orders = jnp.where(is_cosine, azimuth, azimuth - LMAX).astype(jnp.float32)
    phase_angle = orders[None, :, None] * longitude[:, None, :]
    azimuth_terms = jnp.where(is_cosine[None, :, None], jnp.cos(phase_angle), jnp.sin(phase_angle))
    design_t = leg_values * azimuth_terms
    return jnp.einsum("apo,aqo->apq", design_t, whitening, precision=lax.Precision.HIGHEST)


def body(harmonic, legendre, whitening, longitude, observed):
    arc_count = legendre.shape[0]
    azimuth = harmonic.reshape(-1)
    leg_values = legendre.reshape(arc_count, -1, legendre.shape[3])
    portion_t = form_columns(azimuth, leg_values, whitening, longitude)
    white_obs = jnp.einsum("aqo,ao->aq", whitening, observed, precision=lax.Precision.HIGHEST)
    rhs_part = jnp.einsum(
        "apq,aq->p", portion_t, white_obs, precision=lax.Precision.HIGHEST
    ).reshape(1, -1)
    row_width = portion_t.shape[1] * lax.axis_size("col")
    groups_per = lax.axis_size("row") // lax.axis_size("col")
    row_index = lax.axis_index("row")
    root_col = row_index // groups_per
    row_offset = row_index % groups_per * row_width
    column_set = lax.all_gather(portion_t, "row", axis=1, tiled=True)
    own_slice = lax.dynamic_slice_in_dim(column_set, row_offset, row_width, 1)
    row_set = from_root(own_slice, "col", root_col)
    tile_sum = jnp.einsum("aio,ajo->ij", row_set, column_set, precision=lax.Precision.HIGHEST)
    return (tile_sum, rhs_part)


def solution(mesh):
    in_specs = (P("col", "row"), P(None, "col", "row", None), P(), P(), P())
    out_specs = (P("row", "col"), P("col", "row"))
    return jax.shard_map(body, mesh=mesh, in_specs=in_specs, out_specs=out_specs, check_vma=False)
```

profile of v0, /device:TPU:6, one launch (start us, length us, event | category | flops | bytes accessed | tf_op | source)
XLA Modules:
  0.0 159.6 jit_solution(14235089013702268885)
XLA Ops:
  7.2 0.0 copy-start
  7.2 0.0 all-gather.2.cloned.1.call-start
  7.2 0.8 fusion.11
  8.0 0.7 bitcast_compare_fusion
  8.7 0.1 copy-done
  8.8 5.9 %fusion.2 = f32[2,128,512]{2,1,0:T(8,128)} fusion(f32[2,512,512]{2,1,0:T(8,128)S(1)} %copy-done, f32[2,1,128,512]{3,2,1,0:T(8,128)} %param.6, f32[2,512]{1,0:T(2,128)} %param.8, f32[128]{0:T(128)S(1)} %fusion.11, pred[128]{0:T(512)(128)(4,1)S(1)} %bitcast_compare_fusion), kind=kOutput, calls=%fused_computation.7 | convolution fusion | flops 805699584 | bytes 3150464 | tf_op jit(solution)/shard_map/apo,aqo->apq/dot_general | solution.py:20
  14.7 0.0 all-gather.2.cloned.1.call-update
  14.7 0.0 all-reduce.2.cloned.1.call-start
  14.8 37.1 %all-gather.2.cloned.1.call-done = f32[2,1024,512]{2,1,0:T(8,128)} async-done(((f32[2,128,512]{2,1,0:T(8,128)}), f32[2,1024,512]{2,1,0:T(8,128)}) %all-gather.2.cloned.1.call-update) | async-done | bytes 4194320 | tf_op jit(solution)/shard_map/all_gather | solution.py:37
  51.8 3.1 %dynamic-slice_select_fusion = f32[2,512,512]{2,1,0:T(8,128)} fusion(f32[2,1024,512]{2,1,0:T(8,128)} %all-gather.2.cloned.1.call-done, s32[]{:T(128)S(6)} %select_n.39, pred[]{:T(512)S(6)} %eq.5), kind=kLoop, calls=%fused_computation | loop fusion | flops 524288 | bytes 4194309 | tf_op jit(solution)/shard_map/jit(_where)/select_n | solution.py:10
  54.9 0.0 copy-start.2
  55.0 0.0 copy-start.1
  55.0 0.0 all-reduce.2.cloned.1.call-update
  55.0 0.7 copy-done.2
  55.6 1.9 %fusion.9 = f32[2,1,512]{2,1,0:T(1,128)S(1)} fusion(f32[2,512,512]{2,1,0:T(8,128)S(1)} %copy-done, f32[2,512,1]{1,0,2:T(2,128)S(1)} %bitcast.27), kind=kOutput, calls=%fused_computation.14 | convolution fusion | flops 6291456 | bytes 2105344 | tf_op jit(solution)/shard_map/aqo,ao->aq/dot_general | solution.py:28
  57.5 0.0 copy-done.1
  57.5 1.0 convolution_bitcast_fusion.1
  58.6 84.0 %all-reduce.2.cloned.1.call-done = f32[2,512,512]{2,1,0:T(8,128)} async-done(((f32[2,512,512]{2,1,0:T(8,128)}), f32[2,512,512]{2,1,0:T(8,128)}) %all-reduce.2.cloned.1.call-update) | async-done | bytes 2097168 | tf_op jit(solution)/shard_map/psum | solution.py:11
  142.6 10.3 %convolution_bitcast_fusion = f32[512,1024]{1,0:T(8,128)} fusion(f32[2,512,512]{2,1,0:T(8,128)} %all-reduce.2.cloned.1.call-done, f32[2,1024,512]{2,1,0:T(8,128)} %all-gather.2.cloned.1.call-done), kind=kOutput, calls=%fused_computation.1 | convolution fusion | flops 6442450944 | bytes 8388608 | tf_op jit(solution)/shard_map/aio,ajo->ij/dot_general | solution.py:40
  (1 shorter events, 0.0 us)
Async XLA Ops:
  7.2 1.6 %copy-start = (f32[2,512,512]{2,1,0:T(8,128)S(1)}, f32[2,512,512]{2,1,0:T(8,128)}, u32[]{:S(2)}) copy-start(f32[2,512,512]{2,1,0:T(8,128)} %param.7) | copy-start | bytes 6291460
  7.2 44.6 %all-gather.2.cloned.1.call-start = ((), (), s32[]{:S(2)}) async-start(), calls=%async_computation | async-start | bytes 4718592 | tf_op jit(solution)/shard_map/all_gather | solution.py:37
  14.7 127.9 %all-reduce.2.cloned.1.call-start = ((), (), s32[]{:S(2)}) async-start(), calls=%async_computation.1 | async-start | bytes 4194304 | tf_op jit(solution)/shard_map/psum | solution.py:11
  54.9 0.7 copy-start.2
  55.0 2.6 %copy-start.1 = (f32[2,128,512]{2,1,0:T(8,128)S(1)}, f32[2,128,512]{2,1,0:T(8,128)}, u32[]{:S(2)}) copy-start(f32[2,128,512]{2,1,0:T(8,128)} %fusion.2) | copy-start | bytes 1572868
Sparse Core Ops, SparseCore 0:
  14.8 36.9 all-gather.1
  55.1 87.4 all-reduce.1
where the time goes:
time: 161 us; the launch traced here: 160 us
  waiting for transfers between devices  121 us (75%)
  matrix products  19 us (12%)
  between operations  14.1 us (9%)
  other arithmetic  4.59 us (3%)
    psum x1, waiting for transfers between devices, from_root(): return lax.psum(kept, axis)  84 us
    all_gather x1, waiting for transfers between devices, body(): column_set = lax.all_gather(portion_t, 'row', axis=1, tiled=True)  37.1 us
    dot_general x1, matrix products, body(): jnp.einsum('aio,ajo->ij', row_set, column_set, precision=lax.Precision.HI...  10.3 us
    dot_general x1, matrix products, form_columns(): jnp.einsum('apo,aqo->apq', design_t, whitening, precision=lax.Precision.H...  5.88 us
  transfers between devices with their start and end apart: 2, of which 2 were waited for; matrix products, arithmetic and copies ran while one was open for 2% of the time, Pallas kernels for 0%

commit v1 on v0

v1 whole, which is shorter than its diff:
```python
import jax
import jax.numpy as jnp
from jax import lax
from jax.experimental import pallas as pl
from jax.experimental.pallas import tpu as pltpu
from jax.sharding import PartitionSpec as P

LMAX = 156
CHUNKS = 4
MESH = pl.DeviceIdType.MESH


def azimuth_wave(orders, is_sine, longitude):
    angle = orders * longitude
    turns = jnp.floor(angle * 0.6366197723675814 + 0.5)
    rest = angle - turns * 1.5703125
    rest = rest - turns * 4.837512969970703125e-4
    rest = rest - turns * 7.54978995489188216e-8
    sq = rest * rest
    sine = rest + rest * sq * (-1.6666654611e-1 + sq * (8.3321608736e-3 - 1.9515295891e-4 * sq))
    cosine = 1.0 - 0.5 * sq + sq * sq * (
        4.166664568298827e-2 + sq * (-1.388731625493765e-3 + 2.443315711809948e-5 * sq)
    )
    quarter = turns.astype(jnp.int32) - is_sine
    value = jnp.where((quarter & 1) == 1, sine, cosine)
    return jnp.where(((quarter + 1) & 2) == 2, -value, value)


def split(value):
    high = value.astype(jnp.bfloat16)
    return high, (value - high.astype(jnp.float32)).astype(jnp.bfloat16)


def dot_t(a, b):
    return lax.dot_general(a, b, (((1,), (1,)), ((), ())), preferred_element_type=jnp.float32)


def dot3(a_high, a_low, b_high, b_low):
    return dot_t(a_high, b_low) + dot_t(a_low, b_high) + dot_t(a_high, b_high)


def kernel(
    planes,
    harmonic_ref, leg_ref, whitening_ref, longitude_ref, observed_ref,
    normal_ref, rhs_ref,
    cols, rows, col_high, col_low, row_high, row_low,
    s_x, s_y, s_d, s_c, s_up, s_dn,
    r_x, r_y, r_d, r_c, r_z,
):
    arcs, width, obs = leg_ref.shape
    per_arc = CHUNKS // arcs
    me = lax.axis_index("row")
    z = lax.axis_index("col")
    y, x, core = me // 4, (me // 2) % 2, me % 2
    chip = me // 2

    def at(yy, xx, cc):
        return 4 * yy + 2 * xx + cc

    near_x = at(y, 1 - x, core)
    near_y = at(1 - y, x, core)
    across = at(1 - y, 1 - x, core)
    twin = at(y, x, 1 - core)
    mine = (me, near_x, near_y, across)
    other = (twin, at(y, 1 - x, 1 - core), at(1 - y, x, 1 - core), at(1 - y, 1 - x, 1 - core))
    low_z, high_z = jnp.maximum(z - 1, 0), jnp.minimum(z + 1, planes - 1)

    barrier = pltpu.get_barrier_semaphore()
    for peer in (near_x, near_y, twin):
        pl.semaphore_signal(barrier, inc=1, device_id={"row": peer}, device_id_type=MESH)

    @pl.when(z > 0)
    def _():
        pl.semaphore_signal(barrier, inc=1, device_id={"col": low_z}, device_id_type=MESH)

    @pl.when(z < planes - 1)
    def _():
        pl.semaphore_signal(barrier, inc=1, device_id={"col": high_z}, device_id_type=MESH)

    code = jnp.transpose(jnp.broadcast_to(harmonic_ref[...], (width, width)))[:, :1]
    is_sine = jnp.where(code > LMAX, 1, 0)
    orders = (code - LMAX * is_sine).astype(jnp.float32)
    rows_per = width // per_arc
    rhs = jnp.zeros((8, width), jnp.float32)
    for a in range(arcs):
        wave = azimuth_wave(orders, is_sine, longitude_ref[a : a + 1, :])
        d_high, d_low = split(leg_ref[a] * wave)
        w_high, w_low = split(whitening_ref[a])
        part = dot3(d_high, d_low, w_high, w_low)
        for i in range(per_arc):
            cols[me, a * per_arc + i] = part[i * rows_per : (i + 1) * rows_per]
        o_high, o_low = split(jnp.broadcast_to(observed_ref[a : a + 1, :], (8, obs)))
        g_high, g_low = split(dot3(o_high, o_low, w_high, w_low))
        p_high, p_low = split(part)
        rhs = rhs + dot3(g_high, g_low, p_high, p_low)
    rhs_ref[...] = rhs[:1]

    inner = jnp.where(z > 0, 1, 0) + jnp.where(z < planes - 1, 1, 0)
    pl.semaphore_wait(barrier, 3 + inner)

    def copy(src, dst, s, r, **device):
        return pltpu.make_async_remote_copy(
            src_ref=src, dst_ref=dst, send_sem=s, recv_sem=r, device_id=device, device_id_type=MESH
        )

    def block(slot, c):
        return cols.at[slot, c]

    def to_x(c):
        return copy(block(me, c), block(me, c), s_x.at[c], r_x.at[c], row=near_x)

    def to_y(c):
        return copy(block(me, c), block(me, c), s_y.at[c], r_y.at[c], row=near_y)

    def to_across(c):
        if c < CHUNKS // 2:
            return copy(block(near_x, c), block(near_x, c), s_d.at[c], r_d.at[c], row=near_y)
        return copy(block(near_y, c), block(near_y, c), s_d.at[c], r_d.at[c], row=near_x)

    def to_twin(j, c):
        return copy(block(mine[j], c), block(mine[j], c), s_c.at[j, c], r_c.at[j, c], row=twin)

    def wait_x(c):
        copy(block(near_x, c), block(near_x, c), s_x.at[c], r_x.at[c], row=near_x).wait_recv()

    def wait_y(c):
        copy(block(near_y, c), block(near_y, c), s_y.at[c], r_y.at[c], row=near_y).wait_recv()

    def wait_across(c):
        copy(block(across, c), block(across, c), s_d.at[c], r_d.at[c], row=near_x).wait_recv()

    def wait_twin(j, c):
        copy(block(other[j], c), block(other[j], c), s_c.at[j, c], r_c.at[j, c], row=twin).wait_recv()

    source = z == chip
    own_half = y == core
    goes_up = (z >= chip) & (z < planes - 1)
    goes_down = (z <= chip) & (z > 0)
    far_y = y + core - 2 * y * core
    line_y = y + far_y - 2 * y * far_y

    def line_slot(q):
        xx = x if q < 2 else 1 - x
        cc = core if q % 2 == 0 else 1 - core
        return at(line_y, xx, cc)

    def up(src, q, c):
        return copy(src, rows.at[q, c], s_up.at[q, c], r_z.at[q, c], col=high_z)

    def down(src, q, c):
        return copy(src, rows.at[q, c], s_dn.at[q, c], r_z.at[q, c], col=low_z)

    def send_line(src, q, c):
        @pl.when(goes_up)
        def _():
            up(src, q, c).start()

        @pl.when(goes_down)
        def _():
            down(src, q, c).start()

    def from_source(condition, q, c):
        @pl.when(source & condition)
        def _():
            send_line(block(line_slot(q), c), q, c)

    def pass_on(q, c):
        @pl.when(jnp.logical_not(source))
        def _():
            copy(rows.at[q, c], rows.at[q, c], s_up.at[q, c], r_z.at[q, c], col=low_z).wait_recv()
            send_line(rows.at[q, c], q, c)

    far_half = jnp.logical_not(own_half)
    stream = [(2 * h + i, c) for h in range(2) for c in range(CHUNKS) for i in range(2)]
    per_tile = width * 2

    def convert_cols(slot):
        for c in range(CHUNKS):
            a, i = c // per_arc, c % per_arc
            high, low = split(cols[slot, c])
            start = pl.multiple_of(slot * width + i * rows_per, rows_per)
            col_high[pl.ds(start, rows_per), pl.ds(a * obs, obs)] = high
            col_low[pl.ds(start, rows_per), pl.ds(a * obs, obs)] = low

    def convert_rows(half):
        def put(q, c, value):
            a, i = c // per_arc, c % per_arc
            high, low = split(value)
            start = (line_slot(q) % 2) * width + i * rows_per
            start = pl.multiple_of(start, rows_per)
            row_high[pl.ds(start, rows_per), pl.ds(a * obs, obs)] = high
            row_low[pl.ds(start, rows_per), pl.ds(a * obs, obs)] = low

        @pl.when(source)
        def _():
            for q in (2 * half, 2 * half + 1):
                for c in range(CHUNKS):
                    put(q, c, cols[line_slot(q), c])

        @pl.when(jnp.logical_not(source))
        def _():
            for q in (2 * half, 2 * half + 1):
                for c in range(CHUNKS):
                    put(q, c, rows[q, c])

    def multiply(half):
        xx = x if half == 0 else 1 - x
        top = pl.multiple_of(xx * per_tile, per_tile)

        def one(j, carry):
            left = pl.multiple_of(j * per_tile, per_tile)
            normal_ref[pl.ds(top, per_tile), pl.ds(left, per_tile)] = dot3(
                row_high[...], row_low[...],
                col_high[pl.ds(left, per_tile), :], col_low[pl.ds(left, per_tile), :],
            )
            return carry

        lax.fori_loop(0, col_high.shape[0] // per_tile, one, 0)

    for c in range(CHUNKS):
        to_x(c).start()
        to_y(c).start()
        to_twin(0, c).start()
        from_source(own_half, 0, c)
    for c in range(CHUNKS):
        wait_twin(0, c)
        from_source(own_half, 1, c)
    convert_cols(me)
    convert_cols(twin)
    done = 0
    for c in range(CHUNKS):
        wait_x(c)
        if c < CHUNKS // 2:
            to_across(c).start()
        to_twin(1, c).start()
        from_source(own_half, 2, c)
        wait_y(c)
        if c >= CHUNKS // 2:
            to_across(c).start()
        to_twin(2, c).start()
        from_source(far_half, 0, c)
        wait_twin(1, c)
        from_source(own_half, 3, c)
        wait_twin(2, c)
        from_source(far_half, 1, c)
        if c > 0:
            pass_on(*stream[done])
            done += 1
    for c in range(CHUNKS):
        wait_across(c)
        to_twin(3, c).start()
        from_source(far_half, 2, c)
        wait_twin(3, c)
        from_source(far_half, 3, c)
        pass_on(*stream[done])
        done += 1
    for slot in (mine[1], mine[2], mine[3], other[1], other[2], other[3]):
        convert_cols(slot)
    while done < 2 * CHUNKS:
        pass_on(*stream[done])
        done += 1
    convert_rows(0)
    multiply(0)
    while done < 4 * CHUNKS:
        pass_on(*stream[done])
        done += 1
    convert_rows(1)
    multiply(1)

    for c in range(CHUNKS):
        to_x(c).wait_send()
        to_y(c).wait_send()
        to_across(c).wait_send()
        for j in range(4):
            to_twin(j, c).wait_send()

    @pl.when(goes_up)
    def _():
        for q, c in stream:
            up(rows.at[q, c], q, c).wait_send()

    @pl.when(goes_down)
    def _():
        for q, c in stream:
            down(rows.at[q, c], q, c).wait_send()


def fused(row_count, planes):
    def body(harmonic, legendre, whitening, longitude, observed):
        arcs, _, width, obs = legendre.shape
        depth = arcs * obs
        tall = row_count * width
        chunk_rows = arcs * width // CHUNKS
        dma = pltpu.SemaphoreType.DMA
        vmem = pl.BlockSpec(memory_space=pltpu.VMEM)
        normal, rhs = pl.pallas_call(
            lambda *refs: kernel(planes, *refs),
            out_shape=(
                jax.ShapeDtypeStruct((planes * width, tall), jnp.float32),
                jax.ShapeDtypeStruct((1, width), jnp.float32),
            ),
            in_specs=[vmem] * 5,
            out_specs=(vmem, vmem),
            scratch_shapes=[
                pltpu.VMEM((row_count, CHUNKS, chunk_rows, obs), jnp.float32),
                pltpu.VMEM((4, CHUNKS, chunk_rows, obs), jnp.float32),
                pltpu.VMEM((tall, depth), jnp.bfloat16),
                pltpu.VMEM((tall, depth), jnp.bfloat16),
                pltpu.VMEM((2 * width, depth), jnp.bfloat16),
                pltpu.VMEM((2 * width, depth), jnp.bfloat16),
                dma((CHUNKS,)), dma((CHUNKS,)), dma((CHUNKS,)), dma((4, CHUNKS)),
                dma((4, CHUNKS)), dma((4, CHUNKS)),
                dma((CHUNKS,)), dma((CHUNKS,)), dma((CHUNKS,)), dma((4, CHUNKS)),
                dma((4, CHUNKS)),
            ],
            compiler_params=pltpu.CompilerParams(
                collective_id=0, has_side_effects=True, vmem_limit_bytes=48 * 1024 * 1024
            ),
            name="normal_tile",
        )(harmonic, legendre.reshape(arcs, width, obs), whitening, longitude, observed)
        return normal, rhs

    return body


def general(harmonic, legendre, whitening, longitude, observed):
    arcs = legendre.shape[0]
    azimuth = harmonic.reshape(-1)
    leg = legendre.reshape(arcs, -1, legendre.shape[3])
    is_sine = jnp.where(azimuth > LMAX, 1, 0)
    orders = (azimuth - LMAX * is_sine).astype(jnp.float32)
    wave = azimuth_wave(orders[None, :, None], is_sine[None, :, None], longitude[:, None, :])
    high = lax.Precision.HIGH
    portion = jnp.einsum("apo,aqo->apq", leg * wave, whitening, precision=high)
    white_obs = jnp.einsum("aqo,ao->aq", whitening, observed, precision=high)
    rhs = jnp.einsum("apq,aq->p", portion, white_obs, precision=high).reshape(1, -1)
    row_width = portion.shape[1] * lax.axis_size("col")
    groups = lax.axis_size("row") // lax.axis_size("col")
    row_index = lax.axis_index("row")
    column_set = lax.all_gather(portion, "row", axis=1, tiled=True)
    own = lax.dynamic_slice_in_dim(column_set, row_index % groups * row_width, row_width, 1)
    kept = jnp.where(lax.axis_index("col") == row_index // groups, own, 0)
    row_set = lax.psum(kept, "col")
    return jnp.einsum("aio,ajo->ij", row_set, column_set, precision=high), rhs


def solution(mesh):
    in_specs = (P("col", "row"), P(None, "col", "row", None), P(), P(), P())
    out_specs = (P("row", "col"), P("col", "row"))
    row_count, planes = mesh.shape["row"], mesh.shape["col"]
    cube = row_count == 2 ** 3 and row_count == 2 * planes
    body = fused(row_count, planes) if cube else general
    return jax.shard_map(body, mesh=mesh, in_specs=in_specs, out_specs=out_specs, check_vma=False)
```

time: 161 us -> 76.5 us (0.48)
  waiting for transfers between devices: 121 us -> 0 us
  Pallas kernels: 0 us -> 69.1 us
  matrix products: 19 us -> 0 us
  between operations: 14.1 us -> 0.65 us
  local copies, waits for them, and re-layouts: 0.77 us -> 6.48 us
  other arithmetic: 4.59 us -> 0 us
    psum x1 -> x0, waiting for transfers between devices: 84 us -> none  [from_root(): return lax.psum(kept, axis)]
    pallas_call x0 -> x1, Pallas kernels: none -> 69.1 us  [body(): pl.pallas_call(lambda *refs: kernel(planes, *refs), out_shape=(jax.ShapeD...]
    all_gather x1 -> x0, waiting for transfers between devices: 37.1 us -> none  [body(): column_set = lax.all_gather(portion_t, 'row', axis=1, tiled=True)]
    dot_general x4 -> x0, matrix products: 19 us -> none  [the longest x1 10.3 us: body(): jnp.einsum('aio,ajo->ij', row_set, column_set, precision=lax.Precision.HI...]
    unnamed x6 -> x12, local copies, waits for them, and re-layouts: 0.76 us -> 6.48 us
    select_n x1 -> x0, other arithmetic: 3.13 us -> none  [from_root(): jnp.where(lax.axis_index(axis) == source, value, 0).astype(value.dtype)]
  transfers between devices with their start and end apart: 2 -> 0, of which waited for: 2 -> 0; matrix products, arithmetic and copies ran while one was open for 2% -> 0% of each run, Pallas kernels for 0% -> 0%
where the time goes in v1:
time: 76.5 us; the launch traced here: 76.3 us
  Pallas kernels  69.1 us (90%)
  local copies, waits for them, and re-layouts  6.48 us (8%)
    pallas_call x1, Pallas kernels, body(): pl.pallas_call(lambda *refs: kernel(planes, *refs), out_shape=(jax.ShapeD...  69.1 us
    unnamed x12, local copies, waits for them, and re-layouts  6.48 us

profile of v1, /device:TPU:6, one launch (start us, length us, event | category | flops | bytes accessed | tf_op | source)
XLA Modules:
  0.0 76.3 jit_solution(2046487022352484508)
XLA Ops:
  0.6 0.0 copy-start
  0.6 1.6 %copy-done = f32[2,512,512]{2,1,0:T(8,128)S(1)} copy-done((f32[2,512,512]{2,1,0:T(8,128)S(1)}, f32[2,512,512]{2,1,0:T(8,128)}, u32[]{:S(2)}) %copy-start) | copy-done | bytes 2097176
  2.2 0.0 copy-start.1
  2.2 1.0 %copy-done.1 = f32[2,1,128,512]{3,2,1,0:T(8,128)S(1)} copy-done((f32[2,1,128,512]{3,2,1,0:T(8,128)S(1)}, f32[2,1,128,512]{3,2,1,0:T(8,128)}, u32[]{:S(2)}) %copy-start.1) | copy-done | bytes 524312
  3.3 0.0 copy-start.2
  3.3 0.7 copy-done.2
  4.0 0.0 copy-start.3
  4.0 0.7 copy-done.3
  4.6 0.0 copy-start.4
  4.6 0.7 copy-done.4
  5.3 69.1 %normal_tile.1 = (f32[512,1024]{1,0:T(8,128)S(1)}, f32[1,128]{1,0:T(1,128)S(1)}) custom-call(s32[1,128]{1,0:T(1,128)S(1)} %copy-done.4, f32[2,128,512]{2,1,0:T(8,128)S(1)} %bitcast.1, f32[2,512,512]{2,1,0:T(8,128)S(1)} %copy-done, f32[2,512]{1,0:T(2,128)S(1)} %copy-done.2, f32[2,512]{1,0:T(2,128)S(1)} %copy-done.3), custom_call_target="tpu_custom_call" | custom-call | tf_op jit(solution)/shard_map/normal_tile/pallas_call | solution.py:296
  74.4 1.3 %copy.9 = f32[512,1024]{1,0:T(8,128)} copy(f32[512,1024]{1,0:T(8,128)S(1)} %get-tuple-element.4) | data formatting | bytes 4194304
  75.8 0.5 copy.10
Async XLA Ops:
  0.6 1.6 %copy-start = (f32[2,512,512]{2,1,0:T(8,128)S(1)}, f32[2,512,512]{2,1,0:T(8,128)}, u32[]{:S(2)}) copy-start(f32[2,512,512]{2,1,0:T(8,128)} %refs_2_.1) | copy-start | bytes 6291460
  2.2 1.0 %copy-start.1 = (f32[2,1,128,512]{3,2,1,0:T(8,128)S(1)}, f32[2,1,128,512]{3,2,1,0:T(8,128)}, u32[]{:S(2)}) copy-start(f32[2,1,128,512]{3,2,1,0:T(8,128)} %param.6) | copy-start | bytes 1572868
  3.3 0.7 copy-start.2
  4.0 0.7 copy-start.3
  4.6 0.7 copy-start.4

commit v2 on v1

--- a/solution.py
+++ b/solution.py
@@ -41,12 +41,22 @@
 
 def kernel(
     planes,
+    harmonic_in, leg_in, whitening_in, longitude_in, observed_in,
+    normal_ref, rhs_ref,
     harmonic_ref, leg_ref, whitening_ref, longitude_ref, observed_ref,
-    normal_ref, rhs_ref,
-    cols, rows, col_high, col_low, row_high, row_low,
-    s_x, s_y, s_d, s_c, s_up, s_dn,
-    r_x, r_y, r_d, r_c, r_z,
+    cols, rows, col_high, col_low, row_high, row_low, side, turn,
+    s_in, s_x, s_y, s_d, s_c, s_up, s_dn, s_side, s_give, s_turn,
+    r_x, r_y, r_d, r_c, r_z, r_side, r_turn,
 ):
+    fetches = [
+        pltpu.make_async_copy(src, dst, s_in.at[n])
+        for n, (src, dst) in enumerate((
+            (harmonic_in, harmonic_ref), (longitude_in, longitude_ref), (observed_in, observed_ref),
+            (leg_in, leg_ref), (whitening_in, whitening_ref),
+        ))
+    ]
+    for fetch in fetches:
+        fetch.start()
     arcs, width, obs = leg_ref.shape
     per_arc = CHUNKS // arcs
     me = lax.axis_index("row")
@@ -66,7 +76,7 @@
     low_z, high_z = jnp.maximum(z - 1, 0), jnp.minimum(z + 1, planes - 1)
 
     barrier = pltpu.get_barrier_semaphore()
-    for peer in (near_x, near_y, twin):
+    for peer in (near_x, near_y, twin, other[1], other[2]):
         pl.semaphore_signal(barrier, inc=1, device_id={"row": peer}, device_id_type=MESH)
 
     @pl.when(z > 0)
@@ -77,6 +87,8 @@
     def _():
         pl.semaphore_signal(barrier, inc=1, device_id={"col": high_z}, device_id_type=MESH)
 
+    for fetch in fetches:
+        fetch.wait()
     code = jnp.transpose(jnp.broadcast_to(harmonic_ref[...], (width, width)))[:, :1]
     is_sine = jnp.where(code > LMAX, 1, 0)
     orders = (code - LMAX * is_sine).astype(jnp.float32)
@@ -96,7 +108,7 @@
     rhs_ref[...] = rhs[:1]
 
     inner = jnp.where(z > 0, 1, 0) + jnp.where(z < planes - 1, 1, 0)
-    pl.semaphore_wait(barrier, 3 + inner)
+    pl.semaphore_wait(barrier, 5 + inner)
 
     def copy(src, dst, s, r, **device):
         return pltpu.make_async_remote_copy(
@@ -144,35 +156,119 @@
         cc = core if q % 2 == 0 else 1 - core
         return at(line_y, xx, cc)
 
+    last = planes - 1
+    by_side = ((z < chip) & (core == 0)) | ((z > chip) & (core == 1))
+    side_x = jnp.where(core == 0, 0, 1)
+    swap = jnp.where(by_side & (x == side_x), 1, 0)
+
     def up(src, q, c):
         return copy(src, rows.at[q, c], s_up.at[q, c], r_z.at[q, c], col=high_z)
 
     def down(src, q, c):
         return copy(src, rows.at[q, c], s_dn.at[q, c], r_z.at[q, c], col=low_z)
 
-    def send_line(src, q, c):
-        @pl.when(goes_up)
-        def _():
-            up(src, q, c).start()
-
-        @pl.when(goes_down)
-        def _():
-            down(src, q, c).start()
+    def rides_up(q):
+        has_side_x = (x == side_x) if q < 2 else (x != side_x)
+        return source & goes_up & jnp.logical_not(has_side_x & (core == 1))
+
+    def rides_down(q):
+        has_side_x = (x == side_x) if q < 2 else (x != side_x)
+        return source & goes_down & jnp.logical_not(has_side_x & (core == 0))
 
     def from_source(condition, q, c):
-        @pl.when(source & condition)
-        def _():
-            send_line(block(line_slot(q), c), q, c)
-
-    def pass_on(q, c):
-        @pl.when(jnp.logical_not(source))
-        def _():
-            copy(rows.at[q, c], rows.at[q, c], s_up.at[q, c], r_z.at[q, c], col=low_z).wait_recv()
-            send_line(rows.at[q, c], q, c)
+        @pl.when(condition & rides_up(q))
+        def _():
+            up(block(line_slot(q), c), q, c).start()
+
+        @pl.when(condition & rides_down(q))
+        def _():
+            down(block(line_slot(q), c), q, c).start()
+
+    relay = jnp.logical_not(source)
+
+    def place(h):
+        return h + swap - 2 * h * swap
+
+    def onward(h):
+        return relay if h == 0 else relay & jnp.logical_not(by_side)
+
+    def pass_on(h, i, c):
+        q = 2 * place(h) + i
+
+        @pl.when(relay)
+        def _():
+            up(rows.at[q, c], q, c).wait_recv()
+
+        @pl.when(onward(h) & goes_up)
+        def _():
+            up(rows.at[q, c], q, c).start()
+
+        @pl.when(onward(h) & goes_down)
+        def _():
+            down(rows.at[q, c], q, c).start()
+
+    on_side = (chip == 0) | (chip == last)
+    level = jnp.where(chip == last, last - z, z)
+    further = jnp.where(chip == 0, low_z, high_z)
+
+    def side_send(t, c):
+        src = block(me, c) if t == 0 else side.at[t - 1, c]
+        return copy(src, side.at[t, c], s_side.at[t, c], r_side.at[t, c], col=further)
+
+    def side_on(t):
+        held = on_side & (level > 0)
+        return held if t == 0 else held & (level + t <= last)
+
+    def give_x(t, c):
+        q = 2 + far_y
+        return copy(side.at[t - 1, c], rows.at[q, c], s_give.at[t - 1, c], r_z.at[q, c], row=at(y, 1 - x, y))
+
+    def give_y(t, c):
+        q = far_y
+        return copy(side.at[t - 1, c], rows.at[q, c], s_give.at[t - 1, c], r_z.at[q, c], row=at(1 - y, x, y))
+
+    def give_turn(t, c):
+        peer = near_x if c < CHUNKS // 2 else near_y
+        return copy(side.at[t - 1, c], turn.at[c], s_give.at[t - 1, c], r_turn.at[c], row=peer)
+
+    gives = ((1, give_x), (2, give_y), (3, give_turn))
+
+    def side_step(t, c):
+        @pl.when(on_side & (level + t <= last))
+        def _():
+            side_send(t - 1, c).wait_recv()
+            if t < last:
+                @pl.when(level > 0)
+                def _():
+                    side_send(t, c).start()
+            for k, give in gives:
+                if k >= t:
+                    @pl.when(level + t == k)
+                    def _():
+                        give(t, c).start()
+
+    def turn_on(c):
+        from_low = (x == 1) if c < CHUNKS // 2 else (x == 0)
+        there = (from_low & (z < last)) | (jnp.logical_not(from_low) & (z > 0))
+        return jnp.logical_not(on_side) & there
+
+    def turn_send(c):
+        if c < CHUNKS // 2:
+            q, peer = 2 + far_y, at(1 - y, x, y)
+        else:
+            q, peer = 3 - far_y, at(y, 1 - x, 1 - y)
+        return copy(turn.at[c], rows.at[q, c], s_turn.at[c], r_z.at[q, c], row=peer)
+
+    def turn_step(c):
+        @pl.when(turn_on(c))
+        def _():
+            copy(turn.at[c], turn.at[c], s_turn.at[c], r_turn.at[c], row=near_x).wait_recv()
+            turn_send(c).start()
 
     far_half = jnp.logical_not(own_half)
-    stream = [(2 * h + i, c) for h in range(2) for c in range(CHUNKS) for i in range(2)]
+    stream = [(h, i, c) for h in range(2) for c in range(CHUNKS) for i in range(2)]
     per_tile = width * 2
+    tiles = col_high.shape[0] // per_tile
 
     def convert_cols(slot):
         for c in range(CHUNKS):
@@ -182,42 +278,47 @@
             col_high[pl.ds(start, rows_per), pl.ds(a * obs, obs)] = high
             col_low[pl.ds(start, rows_per), pl.ds(a * obs, obs)] = low
 
-    def convert_rows(half):
-        def put(q, c, value):
-            a, i = c // per_arc, c % per_arc
+    def convert_rows(h, a):
+        def put(i, c, value):
             high, low = split(value)
-            start = (line_slot(q) % 2) * width + i * rows_per
-            start = pl.multiple_of(start, rows_per)
-            row_high[pl.ds(start, rows_per), pl.ds(a * obs, obs)] = high
-            row_low[pl.ds(start, rows_per), pl.ds(a * obs, obs)] = low
-
-        @pl.when(source)
-        def _():
-            for q in (2 * half, 2 * half + 1):
-                for c in range(CHUNKS):
-                    put(q, c, cols[line_slot(q), c])
-
-        @pl.when(jnp.logical_not(source))
-        def _():
-            for q in (2 * half, 2 * half + 1):
-                for c in range(CHUNKS):
-                    put(q, c, rows[q, c])
-
-    def multiply(half):
-        xx = x if half == 0 else 1 - x
+            cc = core if i == 0 else 1 - core
+            start = pl.multiple_of(cc * width + (c % per_arc) * rows_per, rows_per)
+            row_high[h, pl.ds(start, rows_per), pl.ds(a * obs, obs)] = high
+            row_low[h, pl.ds(start, rows_per), pl.ds(a * obs, obs)] = low
+
+        for i in range(2):
+            for c in range(a * per_arc, (a + 1) * per_arc):
+                @pl.when(source)
+                def _():
+                    put(i, c, cols[line_slot(2 * h + i), c])
+
+                @pl.when(relay)
+                def _():
+                    put(i, c, rows[2 * place(h) + i, c])
+
+    def multiply(h, start, stop, low_a, high_a, add):
+        turned = place(h)
+        xx = x + turned - 2 * x * turned
         top = pl.multiple_of(xx * per_tile, per_tile)
+        depth = slice(low_a * obs, high_a * obs)
 
         def one(j, carry):
             left = pl.multiple_of(j * per_tile, per_tile)
-            normal_ref[pl.ds(top, per_tile), pl.ds(left, per_tile)] = dot3(
-                row_high[...], row_low[...],
-                col_high[pl.ds(left, per_tile), :], col_low[pl.ds(left, per_tile), :],
+            tile = (pl.ds(top, per_tile), pl.ds(left, per_tile))
+            part = dot3(
+                row_high[h, :, depth], row_low[h, :, depth],
+                col_high[pl.ds(left, per_tile), depth], col_low[pl.ds(left, per_tile), depth],
             )
+            normal_ref[tile] = normal_ref[tile] + part if add else part
             return carry
 
-        lax.fori_loop(0, col_high.shape[0] // per_tile, one, 0)
-
-    for c in range(CHUNKS):
+        lax.fori_loop(start, stop, one, 0)
+
+    for c in range(CHUNKS):
+        @pl.when(side_on(0))
+        def _():
+            side_send(0, c).start()
+
         to_x(c).start()
         to_y(c).start()
         to_twin(0, c).start()
@@ -244,8 +345,10 @@
         wait_twin(2, c)
         from_source(far_half, 1, c)
         if c > 0:
+            side_step(1, c - 1)
             pass_on(*stream[done])
             done += 1
+    side_step(1, CHUNKS - 1)
     for c in range(CHUNKS):
         wait_across(c)
         to_twin(3, c).start()
@@ -254,18 +357,30 @@
         from_source(far_half, 3, c)
         pass_on(*stream[done])
         done += 1
-    for slot in (mine[1], mine[2], mine[3], other[1], other[2], other[3]):
-        convert_cols(slot)
+        convert_cols((mine[1], mine[2], other[1], other[2])[c])
+        if c > 0:
+            side_step(2, c - 1)
     while done < 2 * CHUNKS:
         pass_on(*stream[done])
         done += 1
-    convert_rows(0)
-    multiply(0)
-    while done < 4 * CHUNKS:
-        pass_on(*stream[done])
-        done += 1
-    convert_rows(1)
-    multiply(1)
+    side_step(2, CHUNKS - 1)
+    convert_cols(mine[3])
+    convert_cols(other[3])
+    for a in range(arcs):
+        convert_rows(0, a)
+    for c in range(CHUNKS):
+        side_step(3, c)
+        turn_step(c)
+        for _ in range(2):
+            pass_on(*stream[done])
+            done += 1
+        if (c + 1) % per_arc == 0:
+            convert_rows(1, c // per_arc)
+        if c < CHUNKS // 2:
+            multiply(0, tiles * 2 * c // CHUNKS, tiles * 2 * (c + 1) // CHUNKS, 0, arcs, False)
+        elif c == CHUNKS // 2:
+            multiply(1, 0, tiles, 0, arcs // 2, False)
+    multiply(1, 0, tiles, arcs // 2, arcs, True)
 
     for c in range(CHUNKS):
         to_x(c).wait_send()
@@ -274,15 +389,19 @@
         for j in range(4):
             to_twin(j, c).wait_send()
 
-    @pl.when(goes_up)
-    def _():
-        for q, c in stream:
-            up(rows.at[q, c], q, c).wait_send()
-
-    @pl.when(goes_down)
-    def _():
-        for q, c in stream:
-            down(rows.at[q, c], q, c).wait_send()
+    for h, i, c in stream:
+        q = 2 * h + i
+        pl.when(rides_up(q))(lambda: up(rows.at[q, c], q, c).wait_send())
+        pl.when(rides_down(q))(lambda: down(rows.at[q, c], q, c).wait_send())
+        p = 2 * place(h) + i
+        pl.when(onward(h) & goes_up)(lambda: up(rows.at[p, c], p, c).wait_send())
+        pl.when(onward(h) & goes_down)(lambda: down(rows.at[p, c], p, c).wait_send())
+    for c in range(CHUNKS):
+        for t in range(last):
+            pl.when(side_on(t))(lambda: side_send(t, c).wait_send())
+        for t in range(1, last + 1):
+            pl.when(on_side & (level + t <= last))(lambda: give_turn(t, c).wait_send())
+        pl.when(turn_on(c))(lambda: turn_send(c).wait_send())
 
 
 def fused(row_count, planes):
@@ -299,22 +418,30 @@
                 jax.ShapeDtypeStruct((planes * width, tall), jnp.float32),
                 jax.ShapeDtypeStruct((1, width), jnp.float32),
             ),
-            in_specs=[vmem] * 5,
+            in_specs=[pl.BlockSpec(memory_space=pl.ANY)] * 5,
             out_specs=(vmem, vmem),
             scratch_shapes=[
+                pltpu.VMEM((1, width), jnp.int32),
+                pltpu.VMEM((arcs, width, obs), jnp.float32),
+                pltpu.VMEM((arcs, obs, obs), jnp.float32),
+                pltpu.VMEM((arcs, obs), jnp.float32),
+                pltpu.VMEM((arcs, obs), jnp.float32),
                 pltpu.VMEM((row_count, CHUNKS, chunk_rows, obs), jnp.float32),
                 pltpu.VMEM((4, CHUNKS, chunk_rows, obs), jnp.float32),
                 pltpu.VMEM((tall, depth), jnp.bfloat16),
                 pltpu.VMEM((tall, depth), jnp.bfloat16),
-                pltpu.VMEM((2 * width, depth), jnp.bfloat16),
-                pltpu.VMEM((2 * width, depth), jnp.bfloat16),
+                pltpu.VMEM((2, 2 * width, depth), jnp.bfloat16),
+                pltpu.VMEM((2, 2 * width, depth), jnp.bfloat16),
+                pltpu.VMEM((planes - 1, CHUNKS, chunk_rows, obs), jnp.float32),
+                pltpu.VMEM((CHUNKS, chunk_rows, obs), jnp.float32),
+                dma((5,)), dma((CHUNKS,)), dma((CHUNKS,)), dma((CHUNKS,)), dma((4, CHUNKS)),
+                dma((4, CHUNKS)), dma((4, CHUNKS)),
+                dma((planes - 1, CHUNKS)), dma((planes - 1, CHUNKS)), dma((CHUNKS,)),
                 dma((CHUNKS,)), dma((CHUNKS,)), dma((CHUNKS,)), dma((4, CHUNKS)),
-                dma((4, CHUNKS)), dma((4, CHUNKS)),
-                dma((CHUNKS,)), dma((CHUNKS,)), dma((CHUNKS,)), dma((4, CHUNKS)),
-                dma((4, CHUNKS)),
+                dma((4, CHUNKS)), dma((planes - 1, CHUNKS)), dma((CHUNKS,)),
             ],
             compiler_params=pltpu.CompilerParams(
-                collective_id=0, has_side_effects=True, vmem_limit_bytes=48 * 1024 * 1024
+                collective_id=0, has_side_effects=True, vmem_limit_bytes=56 * 1024 * 1024
             ),
             name="normal_tile",
         )(harmonic, legendre.reshape(arcs, width, obs), whitening, longitude, observed)

time: 76.5 us -> 72.6 us (0.949)
  local copies, waits for them, and re-layouts: 6.48 us -> 3.67 us
  Pallas kernels: 69.1 us -> 68.1 us
    unnamed x12 -> x4, local copies, waits for them, and re-layouts: 6.48 us -> 3.67 us
    pallas_call x1, Pallas kernels: 69.1 us -> 68.1 us  [body(): pl.pallas_call(lambda *refs: kernel(planes, *refs), out_shape=(jax.ShapeD...]
where the time goes in v2:
time: 72.6 us; the launch traced here: 72.4 us
  Pallas kernels  68.1 us (94%)
  local copies, waits for them, and re-layouts  3.67 us (5%)
    pallas_call x1, Pallas kernels, body(): pl.pallas_call(lambda *refs: kernel(planes, *refs), out_shape=(jax.ShapeD...  68.1 us
    unnamed x4, local copies, waits for them, and re-layouts  3.67 us

profile of v2, /device:TPU:6, one launch (start us, length us, event | category | flops | bytes accessed | tf_op | source)
XLA Modules:
  0.0 72.4 jit_solution(16196544819452612760)
XLA Ops:
  0.6 68.1 %normal_tile.1 = (f32[512,1024]{1,0:T(8,128)}, f32[1,128]{1,0:T(1,128)}) custom-call(s32[1,128]{1,0:T(1,128)} %refs_0_.1, f32[2,128,512]{2,1,0:T(8,128)} %bitcast.1, f32[2,512,512]{2,1,0:T(8,128)} %refs_2_.1, f32[2,512]{1,0:T(2,128)} %refs_3_.1, f32[2,512]{1,0:T(2,128)} %refs_4_.1), custom_call_target="tpu_custom_call" | custom-call | tf_op jit(solution)/shard_map/normal_tile/pallas_call | solution.py:415
  68.7 0.0 copy-start
  68.7 3.2 %copy.9 = f32[512,1024]{1,0:T(8,128)} copy(f32[512,1024]{1,0:T(8,128)} %get-tuple-element.4) | data formatting | bytes 4194304
  71.9 0.0 copy-done
  71.9 0.5 copy.10
Async XLA Ops:
  68.7 3.2 %copy-start = (f32[1,128]{1,0:T(1,128)S(1)}, f32[1,128]{1,0:T(1,128)}, u32[]{:S(2)}) copy-start(f32[1,128]{1,0:T(1,128)} %get-tuple-element.5) | copy-start | bytes 1540

commit v3 on v2

--- a/solution.py
+++ b/solution.py
@@ -370,10 +370,10 @@
         convert_rows(0, a)
     for c in range(CHUNKS):
         side_step(3, c)
-        turn_step(c)
         for _ in range(2):
             pass_on(*stream[done])
             done += 1
+        turn_step(c)
         if (c + 1) % per_arc == 0:
             convert_rows(1, c // per_arc)
         if c < CHUNKS // 2:

time: 72.6 us -> 73.8 us (1.017)
  Pallas kernels: 68.1 us -> 69.2 us
    pallas_call x1, Pallas kernels: 68.1 us -> 69.2 us  [body(): pl.pallas_call(lambda *refs: kernel(planes, *refs), out_shape=(jax.ShapeD...]
where the time goes in v3:
time: 73.8 us; the launch traced here: 73.6 us
  Pallas kernels  69.2 us (94%)
  local copies, waits for them, and re-layouts  3.67 us (5%)
    pallas_call x1, Pallas kernels, body(): pl.pallas_call(lambda *refs: kernel(planes, *refs), out_shape=(jax.ShapeD...  69.2 us
    unnamed x4, local copies, waits for them, and re-layouts  3.67 us

profile of v3, /device:TPU:6, one launch (start us, length us, event | category | flops | bytes accessed | tf_op | source)
XLA Modules:
  0.0 73.6 jit_solution(14889871089985283224)
XLA Ops:
  0.6 69.2 %normal_tile.1 = (f32[512,1024]{1,0:T(8,128)}, f32[1,128]{1,0:T(1,128)}) custom-call(s32[1,128]{1,0:T(1,128)} %refs_0_.1, f32[2,128,512]{2,1,0:T(8,128)} %bitcast.1, f32[2,512,512]{2,1,0:T(8,128)} %refs_2_.1, f32[2,512]{1,0:T(2,128)} %refs_3_.1, f32[2,512]{1,0:T(2,128)} %refs_4_.1), custom_call_target="tpu_custom_call" | custom-call | tf_op jit(solution)/shard_map/normal_tile/pallas_call | solution.py:415
  69.9 0.0 copy-start
  69.9 3.2 %copy.9 = f32[512,1024]{1,0:T(8,128)} copy(f32[512,1024]{1,0:T(8,128)} %get-tuple-element.4) | data formatting | bytes 4194304
  73.1 0.0 copy-done
  73.1 0.5 copy.10
Async XLA Ops:
  69.9 3.2 %copy-start = (f32[1,128]{1,0:T(1,128)S(1)}, f32[1,128]{1,0:T(1,128)}, u32[]{:S(2)}) copy-start(f32[1,128]{1,0:T(1,128)} %get-tuple-element.5) | copy-start | bytes 1540
